TPU v7x, 512 devices: a whole 4x8x8 slice. The times are simulated.
512 devices in a mesh: row: 16 (over z, core), col: 32 (over y, x).
Axes of the slice: x: 4, y: 8, z: 8, core: 2. Of those that a mesh axis runs over, the one named last changes fastest.
Arguments:
- train_embed: bfloat16 [8192, 256], P(('row', 'col')), may hold values from -16 to 16
- valid_embed: bfloat16 [65536, 256], P(('row', 'col')), may hold values from -16 to 16
- train_labels: int32 [8192], P(('row', 'col')), may hold values from 0 to 99
- valid_labels: int32 [65536], P(('row', 'col')), may hold values from 0 to 99
- pair_level: int32 [100, 100], replicated, may hold values from 0 to 3
- level_cost: float32 [4], replicated, may hold values from 0.05 to 1
Outputs:
- calibrated: float32 [8192], P('row')
All inputs are finite; a program needn't handle non-finite values.
Results may differ from a plain program's by a relative error of at most 0.0003.
Values may be sent and summed in bfloat16 or wider, within the bound.
No kernel may reach another device: no remote copies, remote signals or barrier semaphores. Data moves between devices by JAX's collectives and lax.ppermute only.
A program may use at most 64 MiB of HBM per device.

v0:
```python
import math
import jax
import jax.numpy as jnp
from jax import lax
from jax.sharding import PartitionSpec as P

ITERS = 4
entropy_scale = 0.05


def inner_products(left_rows, right_rows):
    return lax.dot_general(
        left_rows, right_rows, (((1,), (1,)), ((), ())), preferred_element_type=jnp.float32
    )


def squared_norms(embeddings):
    widened = embeddings.astype(jnp.float32)
    return jnp.sum(widened * widened, axis=1)


def class_costs(pair_level, level_cost):
    num_levels = level_cost.shape[0]
    selected = (
        pair_level[:, :, None] == jnp.arange(num_levels, dtype=jnp.int32)[None, None, :]
    ).astype(jnp.float32)
    return jnp.sum(selected * level_cost[None, None, :], axis=2)


def label_costs(row_labels, class_ids, labels_y):
    col_hot = (class_ids[:, None] == labels_y[None, :]).astype(jnp.float32)
    return jnp.dot(
        row_labels, col_hot, precision=lax.Precision.HIGHEST, preferred_element_type=jnp.float32
    )


def shards(train_embed, valid_embed, train_labels, valid_labels, pair_level, level_cost):
    rows_x, labels_x = (
        lax.all_gather(train_embed, "col", axis=0, tiled=True),
        lax.all_gather(train_labels, "col", axis=0, tiled=True),
    )
    width_d = rows_x.shape[1]
    classes = pair_level.shape[0]
    class_table = class_costs(pair_level, level_cost)
    class_ids = jnp.arange(classes, dtype=jnp.int32)
    train_hot = (labels_x[:, None] == class_ids[None, :]).astype(jnp.float32)
    row_labels = jnp.dot(
        train_hot, class_table, precision=lax.Precision.HIGHEST, preferred_element_type=jnp.float32
    )
    train_sq = squared_norms(rows_x)
    cols_y, labels_y = (
        lax.all_gather(valid_embed, "row", axis=0, tiled=True),
        lax.all_gather(valid_labels, "row", axis=0, tiled=True),
    )
    valid_sq = squared_norms(cols_y)
    label_full = label_costs(row_labels, class_ids, labels_y)

    def cost_block(offset, block_cols):
        block_y = lax.dynamic_slice_in_dim(cols_y, offset, block_cols, 0)
        block_sq = lax.dynamic_slice_in_dim(valid_sq, offset, block_cols, 0)
        label_slice = lax.dynamic_slice_in_dim(label_full, offset, block_cols, 1)
        return (
            train_sq[:, None] + block_sq[None, :] - 2.0 * inner_products(rows_x, block_y)
        ) / width_d + label_slice

    row_count = rows_x.shape[0]
    col_count = labels_y.shape[0]
    block_cols = min(512, col_count)
    block_count = col_count // block_cols
    block_ids = jnp.arange(block_count, dtype=jnp.int32)

    def scores(block_index, row_pot, col_pot):
        offset = block_index * block_cols
        cost_tile = cost_block(offset, block_cols)
        block_pot = lax.dynamic_slice_in_dim(col_pot, offset, block_cols, 0)
        return (
            (block_pot[None, :] - cost_tile) / entropy_scale,
            (row_pot[:, None] - cost_tile) / entropy_scale,
        )

    row_pot = jnp.zeros((row_count,), jnp.float32)
    col_pot = jnp.zeros((col_count,), jnp.float32)
    full_rows = row_count * lax.axis_size("row")
    full_cols = col_count * lax.axis_size("col")
    for iteration in range(ITERS):

        def local_peaks(running, block_index, row_pot=row_pot, col_pot=col_pot):
            row_side, col_side = scores(block_index, row_pot, col_pot)
            return (jnp.maximum(running, jnp.max(row_side, axis=1)), jnp.max(col_side, axis=0))

        row_local, col_local = lax.scan(
            local_peaks, jnp.full((row_count,), -jnp.inf, jnp.float32), block_ids
        )
        row_high = lax.pmax(row_local, "col")
        col_high = lax.pmax(col_local.reshape(col_count), "row")

        def local_totals(
            running,
            block_index,
            row_pot=row_pot,
            col_pot=col_pot,
            row_high=row_high,
            col_high=col_high,
        ):
            row_side, col_side = scores(block_index, row_pot, col_pot)
            block_high = lax.dynamic_slice_in_dim(col_high, block_index * block_cols, block_cols, 0)
            return (
                running + jnp.sum(jnp.exp(row_side - row_high[:, None]), axis=1),
                jnp.sum(jnp.exp(col_side - block_high[None, :]), axis=0),
            )

        row_part, col_part = lax.scan(local_totals, jnp.zeros((row_count,), jnp.float32), block_ids)
        row_sum = lax.psum(row_part, "col")
        col_sum = lax.psum(col_part.reshape(col_count), "row")
        row_new = entropy_scale * math.log(full_cols) - entropy_scale * (
            row_high + jnp.log(row_sum)
        )
        col_new = entropy_scale * math.log(full_rows) - entropy_scale * (
            col_high + jnp.log(col_sum)
        )
        row_pot = 0.5 * (row_pot + row_new)
        col_pot = 0.5 * (col_pot + col_new)
    potential_sum = lax.psum(jnp.sum(row_pot), "row")
    return (row_pot * full_rows - potential_sum) / (full_rows - 1)


def solution(mesh):
    placed = (
        P(("row", "col"), None),
        P(("row", "col"), None),
        P(("row", "col")),
        P(("row", "col")),
        P(),
        P(),
    )
    return jax.shard_map(shards, mesh=mesh, in_specs=placed, out_specs=P("row"), check_vma=False)
```

profile of v0, /device:TPU:1, one launch (start us, length us, event | category | flops | bytes accessed | tf_op | source)
XLA Modules:
  0.0 894.9 jit_solution(5116224132933514768)
XLA Ops:
  10.3 17.5 %all-reduce = s32[512]{0:T(512)S(1)} all-reduce(s32[512]{0:T(512)S(1)} %dynamic-update-slice), channel_id=1, replica_groups=mesh['row'=16,'col'=32] {'col'}, use_global_device_ids=true, to_apply=%add | all-reduce | flops 512 | bytes 4096
  27.7 28.0 %all-gather = s32[16,1,128]{2,1,0:T(1,128)S(1)} all-gather(s32[1,1,128]{2,1,0:T(1,128)} %bitcast.194), channel_id=1, replica_groups=mesh['row'=16,'col'=32] {'row'}, dimensions={0}, use_global_device_ids=true | all-gather | bytes 8704 | tf_op jit(solution)/shard_map/all_gather | solution.py:53
  55.7 34.7 %all_gather.12 = bf16[512,256]{1,0:T(8,128)(2,1)S(1)} all-gather(bf16[16,256]{1,0:T(8,128)(2,1)} %param.22), channel_id=1, replica_groups=mesh['row'=16,'col'=32] {'col'}, dimensions={0}, use_global_device_ids=true | all-gather | bytes 270336 | tf_op jit(solution)/shard_map/all_gather | solution.py:39
  97.4 13.7 %while.100 = (s32[]{:T(128)}, f32[512]{0:T(512)S(1)}, f32[4,512]{1,0:T(4,128)S(1)}, f32[512]{0:T(512)S(1)}, s32[4]{0:T(128)S(1)}, /*index=5*/f32[2048]{0:T(1024)...) while((s32[]{:T(128)}, f32[512]{0:T(512)S(1)}, ...), condition=%wide.region_6.7_spmd.clone, body=%wide.region_3.6_spmd.clone.sunk | while | flops 136577024 | bytes 1596617 | solution.py:91
  111.1 36.0 %pmax.50 = f32[2048]{0:T(1024)S(1)} all-reduce(f32[2048]{0:T(1024)S(1)} %bitcast.188), channel_id=1, replica_groups=mesh['row'=16,'col'=32] {'row'}, use_global_device_ids=true, to_apply=%region_8.9 | all-reduce | flops 2048 | bytes 16384 | tf_op jit(solution)/shard_map/pmax | solution.py:95
  147.1 58.1 %pmax.49 = f32[512]{0:T(512)S(1)} all-reduce(f32[512]{0:T(512)S(1)} %get-tuple-element.462), channel_id=1, replica_groups=mesh['row'=16,'col'=32] {'col'}, use_global_device_ids=true, to_apply=%region_7.8 | all-reduce | flops 512 | bytes 4096 | tf_op jit(solution)/shard_map/pmax | solution.py:94
  205.2 14.1 %while.101 = (s32[]{:T(128)}, f32[512]{0:T(512)S(1)}, f32[4,512]{1,0:T(4,128)S(1)}, f32[512]{0:T(512)S(1)}, s32[4]{0:T(128)S(1)}, /*index=5*/f32[2048]{0:T(1024)...) while((s32[]{:T(128)}, f32[512]{0:T(512)S(1)}, ...), condition=%wide.region_12.13_spmd.clone, body=%wide.region_9.12_spmd.clone.sunk | while | flops 137101312 | bytes 1604829 | solution.py:112
  219.3 56.1 %psum.56 = f32[512]{0:T(512)S(1)} all-reduce(f32[512]{0:T(512)S(1)} %get-tuple-element.464), channel_id=1, replica_groups=mesh['row'=16,'col'=32] {'col'}, use_global_device_ids=true, to_apply=%region_13.14 | all-reduce | flops 512 | bytes 4096 | tf_op jit(solution)/shard_map/psum | solution.py:113
  275.5 51.8 %psum.57 = f32[2048]{0:T(1024)S(1)} all-reduce(f32[2048]{0:T(1024)S(1)} %bitcast.189), channel_id=1, replica_groups=mesh['row'=16,'col'=32] {'row'}, use_global_device_ids=true, to_apply=%region_14.15 | all-reduce | flops 2048 | bytes 16384 | tf_op jit(solution)/shard_map/psum | solution.py:114
  327.3 13.7 %while.102 = (s32[]{:T(128)}, f32[512]{0:T(512)S(1)}, f32[4,512]{1,0:T(4,128)S(1)}, s32[4]{0:T(128)S(1)}, f32[2048]{0:T(1024)S(1)}, /*index=5*/f32[512]{0:T(512)...) while((s32[]{:T(128)}, f32[512]{0:T(512)S(1)}, ...), condition=%wide.region_18.19_spmd.clone, body=%wide.region_15.18_spmd.clone.sunk | while | flops 137101312 | bytes 1604829 | solution.py:91
  341.0 24.0 %pmax.52 = f32[2048]{0:T(1024)S(1)} all-reduce(f32[2048]{0:T(1024)S(1)} %bitcast.190), channel_id=1, replica_groups=mesh['row'=16,'col'=32] {'row'}, use_global_device_ids=true, to_apply=%region_20.21 | all-reduce | flops 2048 | bytes 16384 | tf_op jit(solution)/shard_map/pmax | solution.py:95
  365.1 57.4 %pmax.51 = f32[512]{0:T(512)S(1)} all-reduce(f32[512]{0:T(512)S(1)} %get-tuple-element.466), channel_id=1, replica_groups=mesh['row'=16,'col'=32] {'col'}, use_global_device_ids=true, to_apply=%region_19.20 | all-reduce | flops 512 | bytes 4096 | tf_op jit(solution)/shard_map/pmax | solution.py:94
  422.5 14.9 %while.103 = (s32[]{:T(128)}, f32[512]{0:T(512)S(1)}, f32[4,512]{1,0:T(4,128)S(1)}, s32[4]{0:T(128)S(1)}, f32[2048]{0:T(1024)S(1)}, /*index=5*/f32[512]{0:T(512)...) while((s32[]{:T(128)}, f32[512]{0:T(512)S(1)}, ...), condition=%wide.region_24.25_spmd.clone, body=%wide.region_21.24_spmd.clone.sunk | while | flops 137625600 | bytes 1613041 | solution.py:112
  437.4 56.1 %psum.58 = f32[512]{0:T(512)S(1)} all-reduce(f32[512]{0:T(512)S(1)} %get-tuple-element.468), channel_id=1, replica_groups=mesh['row'=16,'col'=32] {'col'}, use_global_device_ids=true, to_apply=%region_25.26 | all-reduce | flops 512 | bytes 4096 | tf_op jit(solution)/shard_map/psum | solution.py:113
  493.6 51.8 %psum.59 = f32[2048]{0:T(1024)S(1)} all-reduce(f32[2048]{0:T(1024)S(1)} %bitcast.191), channel_id=1, replica_groups=mesh['row'=16,'col'=32] {'row'}, use_global_device_ids=true, to_apply=%region_26.27 | all-reduce | flops 2048 | bytes 16384 | tf_op jit(solution)/shard_map/psum | solution.py:114
  545.4 13.5 %while.104 = (s32[]{:T(128)}, f32[512]{0:T(512)S(1)}, f32[4,512]{1,0:T(4,128)S(1)}, s32[4]{0:T(128)S(1)}, f32[2048]{0:T(1024)S(1)}, /*index=5*/f32[512]{0:T(512)...) while((s32[]{:T(128)}, f32[512]{0:T(512)S(1)}, ...), condition=%wide.region_30.31_spmd.clone, body=%wide.region_27.30_spmd.clone.sunk | while | flops 137101312 | bytes 1604829 | solution.py:91
  558.8 24.1 %pmax.54 = f32[2048]{0:T(1024)S(1)} all-reduce(f32[2048]{0:T(1024)S(1)} %bitcast.192), channel_id=1, replica_groups=mesh['row'=16,'col'=32] {'row'}, use_global_device_ids=true, to_apply=%region_32.33 | all-reduce | flops 2048 | bytes 16384 | tf_op jit(solution)/shard_map/pmax | solution.py:95
  582.9 57.4 %pmax.53 = f32[512]{0:T(512)S(1)} all-reduce(f32[512]{0:T(512)S(1)} %get-tuple-element.470), channel_id=1, replica_groups=mesh['row'=16,'col'=32] {'col'}, use_global_device_ids=true, to_apply=%region_31.32 | all-reduce | flops 512 | bytes 4096 | tf_op jit(solution)/shard_map/pmax | solution.py:94
  640.3 15.5 %while.105 = (s32[]{:T(128)}, f32[512]{0:T(512)S(1)}, f32[4,512]{1,0:T(4,128)S(1)}, s32[4]{0:T(128)S(1)}, f32[2048]{0:T(1024)S(1)}, /*index=5*/f32[512]{0:T(512)...) while((s32[]{:T(128)}, f32[512]{0:T(512)S(1)}, ...), condition=%wide.region_36.37_spmd.clone, body=%wide.region_33.36_spmd.clone.sunk | while | flops 137625600 | bytes 1613041 | solution.py:112
  655.8 38.2 %psum.61 = f32[2048]{0:T(1024)S(1)} all-reduce(f32[2048]{0:T(1024)S(1)} %bitcast.193), channel_id=1, replica_groups=mesh['row'=16,'col'=32] {'row'}, use_global_device_ids=true, to_apply=%region_38.39 | all-reduce | flops 2048 | bytes 16384 | tf_op jit(solution)/shard_map/psum | solution.py:114
  707.3 55.7 %pmax.55 = f32[512]{0:T(512)S(1)} all-reduce(f32[512]{0:T(512)S(1)} %get-tuple-element.474), channel_id=1, replica_groups=mesh['row'=16,'col'=32] {'col'}, use_global_device_ids=true, to_apply=%region_42.43 | all-reduce | flops 512 | bytes 4096 | tf_op jit(solution)/shard_map/pmax | solution.py:94
  763.0 13.4 %while.107 = (s32[]{:T(128)}, f32[512]{0:T(512)S(1)}, s32[4]{0:T(128)S(1)}, f32[2048]{0:T(1024)S(1)}, f32[512]{0:T(512)S(1)}, /*index=5*/f32[2048]{0:T(1024)S(1)...) while((s32[]{:T(128)}, f32[512]{0:T(512)S(1)}, ...), condition=%wide.region_45.46_spmd.clone, body=%wide.region_43.45_spmd.clone.sunk | while | flops 136577536 | bytes 1598673 | solution.py:112
  776.4 57.7 %all-reduce.1 = (f32[512]{0:T(512)S(1)}, f32[512]{0:T(512)S(1)}) all-reduce(f32[512]{0:T(512)S(1)} %get-tuple-element.475, f32[512]{0:T(512)S(1)} %get-tuple-element.472), channel_id=1, replica_groups=mesh['row'=16,'col'=32] {'col'}, use_global_device_ids=true, to_apply=%region_46.47 | all-reduce | flops 1024 | bytes 8192 | tf_op jit(solution)/shard_map/psum | solution.py:113
  834.7 52.1 %psum.63 = f32[]{:T(128)} all-reduce(f32[]{:T(128)} %get-tuple-element.1210), channel_id=1, replica_groups=mesh['row'=16,'col'=32] {'row'}, use_global_device_ids=true, to_apply=%region_48.49 | all-reduce | flops 1 | bytes 8 | tf_op jit(solution)/shard_map/psum | solution.py:123
  (235 shorter events, 115.6 us)
Async XLA Ops:
  6.5 89.3 %all-gather.3.cloned.1.call-start = ((), (), s32[]{:S(2)}) async-start(), calls=%async_computation | async-start | bytes 1114112 | tf_op jit(solution)/shard_map/all_gather | solution.py:52
Sparse Core Ops, SparseCore 0:
  9.5 48.0 all-gather.2
where the time goes:
time: 897 us; the launch traced here: 895 us
  blocking collectives  757 us (84%)
  matrix products  68.1 us (8%)
  local copies, waits for them, and re-layouts  28.5 us (3%)
  loops' own time  21.2 us (2%)
  between operations  14.4 us (2%)
    pmax x4, blocking collectives, shards(): row_high = lax.pmax(row_local, 'col')  229 us
    psum x3, blocking collectives, shards(): row_sum = lax.psum(row_part, 'col')  170 us
    psum x3, blocking collectives, shards(): col_sum = lax.psum(col_part.reshape(col_count), 'row')  142 us
    pmax x3, blocking collectives, shards(): col_high = lax.pmax(col_local.reshape(col_count), 'row')  84.1 us
    dot_general x32, matrix products, inner_products(): lax.dot_general(left_rows, right_rows, (((1,), (1,)), ((), ())), preferre...  64 us
    psum x1, blocking collectives, shards(): potential_sum = lax.psum(jnp.sum(row_pot), 'row')  52.1 us
    all_gather x1, blocking collectives, shards(): lax.all_gather(train_embed, 'col', axis=0, tiled=True)  34.7 us
    all_gather x1, blocking collectives, shards(): lax.all_gather(valid_labels, 'row', axis=0, tiled=True)  28 us
  transfers between devices with their start and end apart: 1, of which 0 were waited for; matrix products, arithmetic and copies ran while one was open for 1% of the time, Pallas kernels for 0%

commit v1 on v0

--- a/solution.py
+++ b/solution.py
@@ -6,6 +6,28 @@
 
 ITERS = 4
 entropy_scale = 0.05
+
+
+def laid_out(blocks, dim):
+    blocks = jnp.moveaxis(blocks, 0, dim)
+    dims = blocks.shape
+    return blocks.reshape(*dims[:dim], dims[dim] * dims[dim + 1], *dims[dim + 2 :])
+
+
+def collect(x, axis, dim):
+    count = lax.axis_size(axis)
+    pairs = [(i, (i + 1) % count) for i in range(count)]
+    back = [(b, a) for a, b in pairs]
+    lower, upper = ([], [])
+    for turn in range(count - 1):
+        if turn % 2 == 0:
+            lower.append(lax.ppermute(lower[-1] if lower else x, axis, pairs))
+        else:
+            upper.append(lax.ppermute(upper[-1] if upper else x, axis, back))
+    pieces = jnp.stack([*lower[::-1], x, *upper])
+    shift = lax.axis_index(axis) - len(lower)
+    pieces = pieces[(jnp.arange(count) - shift) % count]
+    return laid_out(pieces, dim)
 
 
 def inner_products(left_rows, right_rows):
@@ -50,7 +72,7 @@
     train_sq = squared_norms(rows_x)
     cols_y, labels_y = (
         lax.all_gather(valid_embed, "row", axis=0, tiled=True),
-        lax.all_gather(valid_labels, "row", axis=0, tiled=True),
+        collect(valid_labels, "row", 0),
     )
     valid_sq = squared_norms(cols_y)
     label_full = label_costs(row_labels, class_ids, labels_y)

time: 897 us -> 903 us (level)
  blocking collectives: 757 us -> 718 us
  starting transfers between devices: 0.01 us -> 38.3 us
    ppermute x0 -> x15, starting transfers between devices: none -> 38.3 us  [the longest x7 31 us: collect(): upper.append(lax.ppermute(upper[-1] if upper else x, axis, back))]
    all_gather x1 -> x0, blocking collectives: 28 us -> none  [shards(): lax.all_gather(valid_labels, 'row', axis=0, tiled=True)]
    pmax x3, blocking collectives: 84.1 us -> 75 us  [shards(): col_high = lax.pmax(col_local.reshape(col_count), 'row')]
  transfers between devices with their start and end apart: 1 -> 16, of which waited for: 0 -> 6; matrix products, arithmetic and copies ran while one was open for 1% -> 1% of each run, Pallas kernels for 0% -> 0%
where the time goes in v1:
time: 903 us; the launch traced here: 902 us
  blocking collectives  718 us (80%)
  matrix products  67.9 us (8%)
  starting transfers between devices  38.3 us (4%)
  local copies, waits for them, and re-layouts  29.7 us (3%)
  loops' own time  21.2 us (2%)
  between operations  14.4 us (2%)
    pmax x4, blocking collectives, shards(): row_high = lax.pmax(row_local, 'col')  229 us
    psum x3, blocking collectives, shards(): row_sum = lax.psum(row_part, 'col')  170 us
    psum x3, blocking collectives, shards(): col_sum = lax.psum(col_part.reshape(col_count), 'row')  142 us
    pmax x3, blocking collectives, shards(): col_high = lax.pmax(col_local.reshape(col_count), 'row')  75 us
    dot_general x32, matrix products, inner_products(): lax.dot_general(left_rows, right_rows, (((1,), (1,)), ((), ())), preferre...  63.8 us
    psum x1, blocking collectives, shards(): potential_sum = lax.psum(jnp.sum(row_pot), 'row')  52.1 us
    all_gather x1, blocking collectives, shards(): lax.all_gather(train_embed, 'col', axis=0, tiled=True)  35.6 us
    ppermute x7, starting transfers between devices, collect(): upper.append(lax.ppermute(upper[-1] if upper else x, axis, back))  31 us
  transfers between devices with their start and end apart: 16, of which 6 were waited for; matrix products, arithmetic and copies ran while one was open for 1% of the time, Pallas kernels for 0%

profile of v1, /device:TPU:1, one launch (start us, length us, event | category | flops | bytes accessed | tf_op | source)
XLA Modules:
  0.0 901.6 jit_solution(12173360365061751318)
XLA Ops:
  18.0 14.9 %all-reduce = s32[512]{0:T(512)S(1)} all-reduce(s32[512]{0:T(512)S(1)} %dynamic-update-slice), channel_id=1, replica_groups=mesh['row'=16,'col'=32] {'col'}, use_global_device_ids=true, to_apply=%add | all-reduce | flops 512 | bytes 4096
  45.1 35.6 %all_gather.9 = bf16[512,256]{1,0:T(8,128)(2,1)S(1)} all-gather(bf16[16,256]{1,0:T(8,128)(2,1)} %param.22), channel_id=1, replica_groups=mesh['row'=16,'col'=32] {'col'}, dimensions={0}, use_global_device_ids=true | all-gather | bytes 270336 | tf_op jit(solution)/shard_map/all_gather | solution.py:61
  113.4 13.7 %while.100 = (s32[]{:T(128)}, f32[512]{0:T(512)S(1)}, f32[4,512]{1,0:T(4,128)S(1)}, f32[512]{0:T(512)S(1)}, s32[4]{0:T(128)S(1)}, /*index=5*/f32[2048]{0:T(1024)...) while((s32[]{:T(128)}, f32[512]{0:T(512)S(1)}, ...), condition=%wide.region_6.7_spmd.clone, body=%wide.region_3.6_spmd.clone.sunk | while | flops 136577024 | bytes 1596617 | solution.py:113
  127.1 26.9 %pmax.50 = f32[2048]{0:T(1024)S(1)} all-reduce(f32[2048]{0:T(1024)S(1)} %bitcast.205), channel_id=1, replica_groups=mesh['row'=16,'col'=32] {'row'}, use_global_device_ids=true, to_apply=%region_8.9 | all-reduce | flops 2048 | bytes 16384 | tf_op jit(solution)/shard_map/pmax | solution.py:117
  154.0 58.1 %pmax.49 = f32[512]{0:T(512)S(1)} all-reduce(f32[512]{0:T(512)S(1)} %get-tuple-element.462), channel_id=1, replica_groups=mesh['row'=16,'col'=32] {'col'}, use_global_device_ids=true, to_apply=%region_7.8 | all-reduce | flops 512 | bytes 4096 | tf_op jit(solution)/shard_map/pmax | solution.py:116
  212.1 14.1 %while.101 = (s32[]{:T(128)}, f32[512]{0:T(512)S(1)}, f32[4,512]{1,0:T(4,128)S(1)}, f32[512]{0:T(512)S(1)}, s32[4]{0:T(128)S(1)}, /*index=5*/f32[2048]{0:T(1024)...) while((s32[]{:T(128)}, f32[512]{0:T(512)S(1)}, ...), condition=%wide.region_12.13_spmd.clone, body=%wide.region_9.12_spmd.clone.sunk | while | flops 137101312 | bytes 1604829 | solution.py:134
  226.2 56.1 %psum.56 = f32[512]{0:T(512)S(1)} all-reduce(f32[512]{0:T(512)S(1)} %get-tuple-element.464), channel_id=1, replica_groups=mesh['row'=16,'col'=32] {'col'}, use_global_device_ids=true, to_apply=%region_13.14 | all-reduce | flops 512 | bytes 4096 | tf_op jit(solution)/shard_map/psum | solution.py:135
  282.2 51.8 %psum.57 = f32[2048]{0:T(1024)S(1)} all-reduce(f32[2048]{0:T(1024)S(1)} %bitcast.206), channel_id=1, replica_groups=mesh['row'=16,'col'=32] {'row'}, use_global_device_ids=true, to_apply=%region_14.15 | all-reduce | flops 2048 | bytes 16384 | tf_op jit(solution)/shard_map/psum | solution.py:136
  334.1 13.7 %while.102 = (s32[]{:T(128)}, f32[512]{0:T(512)S(1)}, f32[4,512]{1,0:T(4,128)S(1)}, s32[4]{0:T(128)S(1)}, f32[2048]{0:T(1024)S(1)}, /*index=5*/f32[512]{0:T(512)...) while((s32[]{:T(128)}, f32[512]{0:T(512)S(1)}, ...), condition=%wide.region_18.19_spmd.clone, body=%wide.region_15.18_spmd.clone.sunk | while | flops 137101312 | bytes 1604829 | solution.py:113
  347.8 24.1 %pmax.52 = f32[2048]{0:T(1024)S(1)} all-reduce(f32[2048]{0:T(1024)S(1)} %bitcast.207), channel_id=1, replica_groups=mesh['row'=16,'col'=32] {'row'}, use_global_device_ids=true, to_apply=%region_20.21 | all-reduce | flops 2048 | bytes 16384 | tf_op jit(solution)/shard_map/pmax | solution.py:117
  371.9 57.4 %pmax.51 = f32[512]{0:T(512)S(1)} all-reduce(f32[512]{0:T(512)S(1)} %get-tuple-element.466), channel_id=1, replica_groups=mesh['row'=16,'col'=32] {'col'}, use_global_device_ids=true, to_apply=%region_19.20 | all-reduce | flops 512 | bytes 4096 | tf_op jit(solution)/shard_map/pmax | solution.py:116
  429.3 14.9 %while.103 = (s32[]{:T(128)}, f32[512]{0:T(512)S(1)}, f32[4,512]{1,0:T(4,128)S(1)}, s32[4]{0:T(128)S(1)}, f32[2048]{0:T(1024)S(1)}, /*index=5*/f32[512]{0:T(512)...) while((s32[]{:T(128)}, f32[512]{0:T(512)S(1)}, ...), condition=%wide.region_24.25_spmd.clone, body=%wide.region_21.24_spmd.clone.sunk | while | flops 137625600 | bytes 1613041 | solution.py:134
  444.2 56.1 %psum.58 = f32[512]{0:T(512)S(1)} all-reduce(f32[512]{0:T(512)S(1)} %get-tuple-element.468), channel_id=1, replica_groups=mesh['row'=16,'col'=32] {'col'}, use_global_device_ids=true, to_apply=%region_25.26 | all-reduce | flops 512 | bytes 4096 | tf_op jit(solution)/shard_map/psum | solution.py:135
  500.3 51.8 %psum.59 = f32[2048]{0:T(1024)S(1)} all-reduce(f32[2048]{0:T(1024)S(1)} %bitcast.208), channel_id=1, replica_groups=mesh['row'=16,'col'=32] {'row'}, use_global_device_ids=true, to_apply=%region_26.27 | all-reduce | flops 2048 | bytes 16384 | tf_op jit(solution)/shard_map/psum | solution.py:136
  552.1 13.4 %while.104 = (s32[]{:T(128)}, f32[512]{0:T(512)S(1)}, f32[4,512]{1,0:T(4,128)S(1)}, s32[4]{0:T(128)S(1)}, f32[2048]{0:T(1024)S(1)}, /*index=5*/f32[512]{0:T(512)...) while((s32[]{:T(128)}, f32[512]{0:T(512)S(1)}, ...), condition=%wide.region_30.31_spmd.clone, body=%wide.region_27.30_spmd.clone.sunk | while | flops 137101312 | bytes 1604829 | solution.py:113
  565.6 24.0 %pmax.54 = f32[2048]{0:T(1024)S(1)} all-reduce(f32[2048]{0:T(1024)S(1)} %bitcast.209), channel_id=1, replica_groups=mesh['row'=16,'col'=32] {'row'}, use_global_device_ids=true, to_apply=%region_32.33 | all-reduce | flops 2048 | bytes 16384 | tf_op jit(solution)/shard_map/pmax | solution.py:117
  589.6 57.4 %pmax.53 = f32[512]{0:T(512)S(1)} all-reduce(f32[512]{0:T(512)S(1)} %get-tuple-element.470), channel_id=1, replica_groups=mesh['row'=16,'col'=32] {'col'}, use_global_device_ids=true, to_apply=%region_31.32 | all-reduce | flops 512 | bytes 4096 | tf_op jit(solution)/shard_map/pmax | solution.py:116
  647.1 15.4 %while.105 = (s32[]{:T(128)}, f32[512]{0:T(512)S(1)}, f32[4,512]{1,0:T(4,128)S(1)}, s32[4]{0:T(128)S(1)}, f32[2048]{0:T(1024)S(1)}, /*index=5*/f32[512]{0:T(512)...) while((s32[]{:T(128)}, f32[512]{0:T(512)S(1)}, ...), condition=%wide.region_36.37_spmd.clone, body=%wide.region_33.36_spmd.clone.sunk | while | flops 137625600 | bytes 1613041 | solution.py:134
  662.5 38.2 %psum.61 = f32[2048]{0:T(1024)S(1)} all-reduce(f32[2048]{0:T(1024)S(1)} %bitcast.210), channel_id=1, replica_groups=mesh['row'=16,'col'=32] {'row'}, use_global_device_ids=true, to_apply=%region_38.39 | all-reduce | flops 2048 | bytes 16384 | tf_op jit(solution)/shard_map/psum | solution.py:136
  700.8 13.1 %while.106 = (s32[]{:T(128)}, f32[512]{0:T(512)S(1)}, s32[4]{0:T(128)S(1)}, f32[2048]{0:T(1024)S(1)}, f32[512]{0:T(512)S(1)}, /*index=5*/f32[2048]{0:T(1024)S(1)...) while((s32[]{:T(128)}, f32[512]{0:T(512)S(1)}, ...), condition=%wide.region_41.42_spmd.clone, body=%wide.region_39.41_spmd.clone.sunk | while | flops 136315392 | bytes 1596617 | solution.py:113
  714.0 55.7 %pmax.55 = f32[512]{0:T(512)S(1)} all-reduce(f32[512]{0:T(512)S(1)} %get-tuple-element.474), channel_id=1, replica_groups=mesh['row'=16,'col'=32] {'col'}, use_global_device_ids=true, to_apply=%region_42.43 | all-reduce | flops 512 | bytes 4096 | tf_op jit(solution)/shard_map/pmax | solution.py:116
  769.7 13.4 %while.107 = (s32[]{:T(128)}, f32[512]{0:T(512)S(1)}, s32[4]{0:T(128)S(1)}, f32[2048]{0:T(1024)S(1)}, f32[512]{0:T(512)S(1)}, /*index=5*/f32[2048]{0:T(1024)S(1)...) while((s32[]{:T(128)}, f32[512]{0:T(512)S(1)}, ...), condition=%wide.region_45.46_spmd.clone, body=%wide.region_43.45_spmd.clone.sunk | while | flops 136577536 | bytes 1598673 | solution.py:134
  783.1 57.7 %all-reduce.1 = (f32[512]{0:T(512)S(1)}, f32[512]{0:T(512)S(1)}) all-reduce(f32[512]{0:T(512)S(1)} %get-tuple-element.475, f32[512]{0:T(512)S(1)} %get-tuple-element.472), channel_id=1, replica_groups=mesh['row'=16,'col'=32] {'col'}, use_global_device_ids=true, to_apply=%region_46.47 | all-reduce | flops 1024 | bytes 8192 | tf_op jit(solution)/shard_map/psum | solution.py:135
  841.4 52.1 %psum.63 = f32[]{:T(128)} all-reduce(f32[]{:T(128)} %get-tuple-element.1123), channel_id=1, replica_groups=mesh['row'=16,'col'=32] {'row'}, use_global_device_ids=true, to_apply=%region_48.49 | all-reduce | flops 1 | bytes 8 | tf_op jit(solution)/shard_map/psum | solution.py:145
  (268 shorter events, 148.0 us)
Async XLA Ops:
  6.5 105.3 %all-gather.2.cloned.1.call-start = ((), (), s32[]{:S(2)}) async-start(), calls=%async_computation | async-start | bytes 1114112 | tf_op jit(solution)/shard_map/all_gather | solution.py:74
  7.3 10.8 %collective-permute-start = (s32[128]{0:T(128)}, s32[128]{0:T(128)S(1)}, u32[]{:S(2)}, u32[]{:S(2)}) collective-permute-start(s32[128]{0:T(128)} %param.25), channel_id=1, source_target_pairs={{0,32},{32,64},{64,96},{96,128},{128,160},{160,192},{192,224},{224... | collective-permute-start | bytes 1544 | tf_op jit(solution)/shard_map/ppermute | solution.py:24
  10.8 22.2 %collective-permute-start.8 = (s32[128]{0:T(128)}, s32[128]{0:T(128)S(1)}, u32[]{:S(2)}, u32[]{:S(2)}) collective-permute-start(s32[128]{0:T(128)} %param.25), channel_id=1, source_target_pairs={{32,0},{64,32},{96,64},{128,96},{160,128},{192,160},{224,192},{256... | collective-permute-start | bytes 1544 | tf_op jit(solution)/shard_map/ppermute | solution.py:26
  18.0 24.1 %collective-permute-start.1 = (s32[128]{0:T(128)S(1)}, s32[128]{0:T(128)S(1)}, u32[]{:S(2)}, u32[]{:S(2)}) collective-permute-start(s32[128]{0:T(128)S(1)} %collective-permute-done), channel_id=1, source_target_pairs={{0,32},{32,64},{64,96},{96,128},{128,160},{160,192},{192,224},{224... | collective-permute-start | bytes 1544 | tf_op jit(solution)/shard_map/ppermute | solution.py:24
  33.0 10.0 %collective-permute-start.9 = (s32[128]{0:T(128)S(1)}, s32[128]{0:T(128)S(1)}, u32[]{:S(2)}, u32[]{:S(2)}) collective-permute-start(s32[128]{0:T(128)S(1)} %collective-permute-done.8), channel_id=1, source_target_pairs={{32,0},{64,32},{96,64},{128,96},{160,128},{192,160},{224,192},{256... | collective-permute-start | bytes 1544 | tf_op jit(solution)/shard_map/ppermute | solution.py:26
  42.1 1.3 collective-permute-start.2
  42.9 37.8 %collective-permute-start.10 = (s32[128]{0:T(128)S(1)}, s32[128]{0:T(128)S(1)}, u32[]{:S(2)}, u32[]{:S(2)}) collective-permute-start(s32[128]{0:T(128)S(1)} %collective-permute-done.9), channel_id=1, source_target_pairs={{32,0},{64,32},{96,64},{128,96},{160,128},{192,160},{224,192},{256... | collective-permute-start | bytes 1544 | tf_op jit(solution)/shard_map/ppermute | solution.py:26
  43.4 50.2 %collective-permute-start.3 = (s32[128]{0:T(128)S(1)}, s32[128]{0:T(128)S(1)}, u32[]{:S(2)}, u32[]{:S(2)}) collective-permute-start(s32[128]{0:T(128)S(1)} %collective-permute-done.2), channel_id=1, source_target_pairs={{0,32},{32,64},{64,96},{96,128},{128,160},{160,192},{192,224},{224... | collective-permute-start | bytes 1544 | tf_op jit(solution)/shard_map/ppermute | solution.py:24
  80.7 13.7 %collective-permute-start.11 = (s32[128]{0:T(128)S(1)}, s32[128]{0:T(128)S(1)}, u32[]{:S(2)}, u32[]{:S(2)}) collective-permute-start(s32[128]{0:T(128)S(1)} %collective-permute-done.10), channel_id=1, source_target_pairs={{32,0},{64,32},{96,64},{128,96},{160,128},{192,160},{224,192},{256... | collective-permute-start | bytes 1544 | tf_op jit(solution)/shard_map/ppermute | solution.py:26
  93.6 1.3 collective-permute-start.4
  94.4 3.0 collective-permute-start.12
  94.9 4.2 collective-permute-start.5
  97.4 3.0 collective-permute-start.13
  99.1 4.2 collective-permute-start.6
  100.3 3.7 collective-permute-start.14
  103.2 3.5 collective-permute-start.7
Sparse Core Ops, SparseCore 0:
  9.5 47.8 all-gather.1
